TPU v7x, 256 devices: a whole 4x4x8 slice. The times are simulated.
256 devices in a mesh: row: 8 (over y, core), col: 32 (over z, x).
Axes of the slice: x: 4, y: 4, z: 8, core: 2. Of those that a mesh axis runs over, the one named last changes fastest.
Arguments:
- ainv: bfloat16 [2, 32, 512, 8, 8, 512], P(None, 'col', None, None, 'row'), may hold values from -6 to 6
- panel: bfloat16 [2, 8, 8, 512, 512], P(None, None, 'row', 'col'), may hold values from -0.03125 to 0.03125
- pattern: int32 [2, 64], replicated, may hold values 0 or 1
- dinv: bfloat16 [2, 512, 512], replicated, may hold values from -6 to 6
Outputs:
- column_blocks: bfloat16 [2, 2, 32, 512, 512], P(None, None, 'col')
- diagonal: bfloat16 [2, 512, 512], replicated
All inputs are finite; a program needn't handle non-finite values.
Results may differ from a plain program's by a relative error of at most 0.0034.
Values may be sent and summed in bfloat16 or wider, within the bound.
No kernel may reach another device: no remote copies, remote signals or barrier semaphores. Data moves between devices by JAX's collectives and lax.ppermute only.
A program may use at most 128 MiB of HBM per device.

v0:
```python
import jax
import jax.numpy as jnp
from jax import lax
from jax.sharding import PartitionSpec as P


def from_root(block, axis, owner):
    block = jnp.where(lax.axis_index(axis) == owner, block, jnp.zeros_like(block))
    return lax.psum(block, axis)


def pick_blocks(pattern, block_ids):
    total = pattern.shape[1]
    select = (jnp.arange(total, dtype=jnp.int32)[None, :] == block_ids[:, None]).astype(jnp.int32)
    return jnp.sum(pattern[:, None, :] * select[None, :, :], axis=2)


def body(ainv, panel, pattern, dinv):
    row_count = lax.axis_size("row")
    col_count = lax.axis_size("col")
    row_at = lax.axis_index("row")
    col_at = lax.axis_index("col")
    ibk = ainv.shape[0]
    width = ainv.shape[2]
    jbk = ainv.shape[3]
    ratio = col_count // row_count
    pieces = lax.all_gather(panel, "col", axis=3, tiled=True)
    gathered = pieces.reshape(2, jbk, width, width)
    keep_cols = pick_blocks(pattern, jnp.arange(jbk, dtype=jnp.int32) * row_count + row_at)
    masked = jnp.where(keep_cols[:, :, None, None] > 0, gathered, jnp.zeros_like(gathered))
    local_inverse = ainv.reshape(ibk * width, jbk * width)
    partial_sum = jnp.einsum(
        "mn,knb->kmb",
        local_inverse,
        masked.reshape(2, jbk * width, width),
        preferred_element_type=jnp.float32,
    )
    keep_rows = pick_blocks(pattern, jnp.arange(ibk, dtype=jnp.int32) * col_count + col_at)
    own_panel = lax.dynamic_index_in_dim(
        masked.reshape(2, ibk, ratio, width, width), col_at // row_count, axis=2, keepdims=False
    )
    holder = col_at % row_count
    shared = from_root(own_panel, "row", holder)
    totals = lax.psum(partial_sum, "row")
    upper = -jnp.where(
        keep_rows[:, :, None, None] > 0,
        totals.reshape(2, ibk, width, width),
        jnp.zeros((2, ibk, width, width), jnp.float32),
    )
    rounded = upper.astype(jnp.bfloat16)
    column_blocks = rounded.reshape(2, ibk, 1, width, width)
    slab = width // row_count
    panel_part = lax.dynamic_slice_in_dim(shared, row_at * slab, slab, 2)
    upper_part = lax.dynamic_slice_in_dim(rounded, row_at * slab, slab, 2)
    term = jnp.einsum(
        "kna,knb->kab",
        panel_part.reshape(2, ibk * slab, width),
        upper_part.reshape(2, ibk * slab, width),
        preferred_element_type=jnp.float32,
    )
    summed = lax.psum(term, ("row", "col"))
    diagonal = (dinv.astype(jnp.float32) - summed).astype(jnp.bfloat16)
    return (column_blocks, diagonal)


def solution(mesh):
    placed = (P(None, "col", None, None, "row", None), P(None, None, "row", "col", None), P(), P())
    return jax.shard_map(
        body,
        mesh=mesh,
        in_specs=placed,
        out_specs=(P(None, None, "col", None, None), P()),
        check_vma=False,
    )
```

profile of v0, /device:TPU:2, one launch (start us, length us, event | category | flops | bytes accessed | tf_op | source)
XLA Modules:
  0.0 545.1 jit_solution(8546062230581940028)
XLA Ops:
  7.2 0.0 all-gather.2.cloned.1.call-start
  7.2 0.7 all-gather.2.cloned.1.call-update
  7.9 0.0 all-reduce.6.cloned.1.call-start
  8.0 0.1 fusion.4
  8.1 0.8 multiply_reduce_fusion
  8.9 0.1 gt.22
  9.0 13.5 %reshape.119 = bf16[1024,4096,1]{1,0,2:T(8,128)(2,1)} reshape(bf16[2,1,512,8,1,512]{5,3,4,2,1,0:T(8,128)(2,1)} %param.4) | data formatting | bytes 16777216 | tf_op jit(solution)/shard_map/reshape | solution.py:31
  22.5 0.1 constant_dynamic-slice_fusion
  22.5 88.1 %all-gather.2.cloned.1.call-done = bf16[2,8,1,512,512]{4,3,1,0,2:T(8,128)(2,1)} async-done(((bf16[2,8,1,16,512]{4,3,1,0,2:T(8,128)(2,1)}), bf16[2,8,1,512,512]{4,3,1,0,2:T(8,128)(2,1)}) %all-gather.2.cloned.1.call-update) | async-done | bytes 8388624 | tf_op jit(solution)/shard_map/all_gather | solution.py:27
  110.6 3.2 fusion.1
  113.8 0.0 all-reduce.6.cloned.1.call-update
  113.8 0.0 all-reduce.4.cloned.1.call-start
  113.8 7.2 %broadcast_select_fusion = bf16[2,8,1,512,512]{4,3,1,0,2:T(8,128)(2,1)} fusion(bf16[2,8,1,512,512]{4,3,1,0,2:T(8,128)(2,1)} %all-gather.2.cloned.1.call-done, pred[2,8]{1,0:T(4,128)(4,1)S(1)} %broadcast_compare_fusion), kind=kLoop, calls=%fused_computation | loop fusion | flops 4194304 | bytes 16777232 | tf_op jit(solution)/shard_map/jit(_where)/select_n | solution.py:30
  121.0 15.3 %convolution_bitcast_fusion = f32[2,1024,512]{1,2,0:T(8,128)} fusion(bf16[2,4096,512]{2,1,0:T(8,128)(2,1)} %bitcast.22, bf16[1024,4096,1]{1,0,2:T(8,128)(2,1)} %reshape.119), kind=kOutput, calls=%fused_computation.2 | convolution fusion | flops 8589934592 | bytes 20971520 | tf_op jit(solution)/shard_map/mn,knb->kmb/dot_general | solution.py:32
  136.3 0.0 copy-start.1
  136.3 0.0 all-reduce.4.cloned.1.call-update
  136.4 0.0 all-reduce.8.cloned.1.call-start
  136.4 0.1 compare_convert_fusion
  136.5 0.5 copy-done.1
  137.0 0.1 multiply_reduce_fusion.1
  137.2 45.9 %all-reduce.6.cloned.1.call-done = bf16[2,2,512,512]{3,2,1,0:T(8,128)(2,1)} async-done(((bf16[2,2,512,512]{3,2,1,0:T(8,128)(2,1)}), bf16[2,2,512,512]{3,2,1,0:T(8,128)(2,1)}) %all-reduce.6.cloned.1.call-update) | async-done | bytes 2097168 | tf_op jit(solution)/shard_map/psum | solution.py:9
  183.1 1.0 constant_dynamic-slice_fusion.1
  184.1 78.8 %all-reduce.4.cloned.1.call-done = f32[2,1024,512]{1,2,0:T(8,128)} async-done(((f32[2,1024,512]{1,2,0:T(8,128)}), f32[2,1024,512]{1,2,0:T(8,128)}) %all-reduce.4.cloned.1.call-update) | async-done | bytes 4194320 | tf_op jit(solution)/shard_map/psum | solution.py:44
  262.9 6.6 %reshape.117 = f32[2,2,512,512]{2,1,3,0:T(2,128)} reshape(f32[2,1024,512]{1,2,0:T(8,128)} %all-reduce.4.cloned.1.call-done) | data formatting | bytes 8388608 | tf_op jit(solution)/shard_map/reshape | solution.py:47
  269.4 2.4 fusion.3
  271.8 0.4 copy.24
  272.2 1.8 fusion.5
  274.0 0.0 all-reduce.8.cloned.1.call-update
  274.0 5.4 copy.28
  279.4 0.0 copy-start
  279.4 4.2 negate_convert_fusion
  283.7 252.0 %all-reduce.8.cloned.1.call-done = f32[2,512,512]{2,1,0:T(8,128)} async-done(((f32[2,512,512]{2,1,0:T(8,128)}), f32[2,512,512]{2,1,0:T(8,128)}) %all-reduce.8.cloned.1.call-update) | async-done | bytes 2097168 | tf_op jit(solution)/shard_map/psum | solution.py:61
  535.7 0.0 copy-done
  535.7 2.9 subtract_convert_fusion
  (4 shorter events, 0.0 us)
Async XLA Ops:
  7.2 103.4 %all-gather.2.cloned.1.call-start = ((), (), s32[]{:S(2)}) async-start(), calls=%async_computation | async-start | bytes 8650752 | tf_op jit(solution)/shard_map/all_gather | solution.py:27
  7.9 175.2 %all-reduce.6.cloned.1.call-start = ((), (), s32[]{:S(2)}) async-start(), calls=%async_computation.2 | async-start | bytes 4194304 | tf_op jit(solution)/shard_map/psum | solution.py:9
  113.8 149.1 %all-reduce.4.cloned.1.call-start = ((), (), s32[]{:S(2)}) async-start(), calls=%async_computation.1 | async-start | bytes 8388608 | tf_op jit(solution)/shard_map/psum | solution.py:44
  136.3 0.7 copy-start.1
  136.4 399.3 %all-reduce.8.cloned.1.call-start = ((), (), s32[]{:S(2)}) async-start(), calls=%async_computation.3 | async-start | bytes 4194304 | tf_op jit(solution)/shard_map/psum | solution.py:61
  279.4 256.2 %copy-start = (bf16[2,512,512]{2,1,0:T(8,128)(2,1)S(1)}, bf16[2,512,512]{2,1,0:T(8,128)(2,1)}, u32[]{:S(2)}) copy-start(bf16[2,512,512]{2,1,0:T(8,128)(2,1)} %param.7) | copy-start | bytes 3145732
Sparse Core Ops, SparseCore 0:
  10.6 99.9 all-gather.1
  113.9 69.1 all-reduce.5
  185.5 77.3 all-reduce.3
  274.1 261.4 all-reduce.7
where the time goes:
time: 546 us; the launch traced here: 545 us
  waiting for transfers between devices  466 us (85%)
  local copies, waits for them, and re-layouts  27.5 us (5%)
  other arithmetic  21 us (4%)
  matrix products  17.1 us (3%)
  between operations  13.8 us (3%)
    psum x1, waiting for transfers between devices, body(): summed = lax.psum(term, ('row', 'col'))  252 us
    all_gather x1, waiting for transfers between devices, body(): pieces = lax.all_gather(panel, 'col', axis=3, tiled=True)  88.1 us
    psum x1, waiting for transfers between devices, body(): totals = lax.psum(partial_sum, 'row')  78.8 us
    psum x1, waiting for transfers between devices, from_root(): return lax.psum(block, axis)  45.9 us
    dot_general x1, matrix products, body(): jnp.einsum('mn,knb->kmb', local_inverse, masked.reshape(2, jbk * width, w...  15.3 us
    reshape x1, local copies, waits for them, and re-layouts, body(): local_inverse = ainv.reshape(ibk * width, jbk * width)  13.5 us
    reshape x2, local copies, waits for them, and re-layouts, body(): totals.reshape(2, ibk, width, width)  12 us
  transfers between devices with their start and end apart: 4, of which 4 were waited for; matrix products, arithmetic and copies ran while one was open for 9% of the time, Pallas kernels for 0%

commit v1 on v0

v1 whole, which is shorter than its diff:
```python
import jax
import jax.numpy as jnp
from jax import lax
from jax.sharding import PartitionSpec as P

BF16 = jnp.bfloat16
F32 = jnp.float32
CORES = 2


def row_pairs(y_size, shift):
    return [(y * CORES + core, (y + shift) % y_size * CORES + core) for y in range(y_size) for core in range(CORES)]


def core_pairs(y_size):
    return [(y * CORES + core, y * CORES + 1 - core) for y in range(y_size) for core in range(CORES)]


def y_groups(y_size):
    return [[y * CORES + core for y in range(y_size)] for core in range(CORES)]


def swap_cores(block, y_size):
    return lax.ppermute(block, "row", core_pairs(y_size))


def gather_y(own, y_at, y_size):
    out = jnp.zeros((y_size,) + own.shape, own.dtype)
    out = lax.dynamic_update_index_in_dim(out, own, y_at, 0)
    for shift in range(1, y_size):
        got = lax.ppermute(own, "row", row_pairs(y_size, shift))
        out = lax.dynamic_update_index_in_dim(out, got, (y_at - shift) % y_size, 0)
    return out.reshape((y_size * own.shape[0],) + own.shape[1:])


def scatter_sum_y(block, y_at, y_size):
    slabs = block.reshape((y_size, block.shape[0] // y_size) + block.shape[1:])
    total = lax.dynamic_index_in_dim(slabs, y_at, 0, keepdims=False)
    for shift in range(1, y_size):
        piece = lax.dynamic_index_in_dim(slabs, (y_at + shift) % y_size, 0, keepdims=False)
        total = total + lax.ppermute(piece, "row", row_pairs(y_size, shift))
    return total


def gather_panel(own):
    kk, jbk, part, width = own.shape
    return lax.all_gather(own, "col", axis=2, tiled=True).reshape(kk, -1, width)


def body(ainv, panel, pattern, dinv):
    row_count = lax.axis_size("row")
    col_count = lax.axis_size("col")
    row_at = lax.axis_index("row")
    col_at = lax.axis_index("col")
    y_size = row_count // CORES
    y_at = row_at // CORES
    core = row_at % CORES
    ibk, width, jbk = ainv.shape[0], ainv.shape[2], ainv.shape[3]
    kk = panel.shape[0]
    ratio = col_count // row_count
    holder = col_at % row_count
    quarter = col_at // row_count

    keep_cols = lax.dynamic_index_in_dim(pattern.reshape(kk, jbk, row_count), row_at, 2, keepdims=False)
    own = panel[:, :, 0]
    own = jnp.where(keep_cols[:, :, None, None] > 0, own, jnp.zeros_like(own))
    masked = gather_panel(own)

    inverse = ainv.reshape(ibk, width, jbk * width)
    mine = lax.dynamic_index_in_dim(inverse, core, 0, keepdims=False)
    theirs = lax.dynamic_index_in_dim(inverse, 1 - core, 0, keepdims=False)
    keep_rows = lax.dynamic_index_in_dim(pattern.reshape(kk, ibk, col_count), col_at, 2, keepdims=False)
    keep_rows = lax.dynamic_index_in_dim(keep_rows, core, 1, keepdims=False)

    blocks = masked.reshape(kk, ibk, ratio, width, width)
    blocks = lax.dynamic_index_in_dim(blocks, quarter, 2, keepdims=False)
    for_me = lax.dynamic_index_in_dim(blocks, core, 1, keepdims=False)
    for_sibling = lax.dynamic_index_in_dim(blocks, 1 - core, 1, keepdims=False)
    from_sibling = swap_cores(for_sibling, y_size)
    lower = jnp.where(holder % CORES == core, for_me, from_sibling)
    slab = width // y_size
    parts = lower.reshape(kk, width, y_size, slab).transpose(2, 0, 1, 3)
    parts = lax.all_to_all(parts, "row", 0, 0, axis_index_groups=y_groups(y_size))
    lower_part = lax.dynamic_index_in_dim(parts, holder // CORES, 0, keepdims=False)

    columns = []
    terms = []
    for k in range(kk):
        sent = swap_cores(jnp.dot(theirs, masked[k], preferred_element_type=F32), y_size)
        both = jnp.dot(mine, masked[k], preferred_element_type=F32) + sent
        total = scatter_sum_y(both, y_at, y_size)
        upper = -jnp.where(keep_rows[k] > 0, total, jnp.zeros_like(total))
        column = gather_y(upper.astype(BF16), y_at, y_size)
        other = swap_cores(column, y_size)
        columns.append(jnp.stack([jnp.where(core == 0, column, other), jnp.where(core == 0, other, column)]))
        term = lax.dot_general(lower_part[k], column, (((0,), (0,)), ((), ())), preferred_element_type=F32)
        half = term.reshape(CORES, slab // CORES, width)
        kept = lax.dynamic_index_in_dim(half, core, 0, keepdims=False)
        given = lax.dynamic_index_in_dim(half, 1 - core, 0, keepdims=False)
        terms.append(kept + swap_cores(given, y_size))
    column_blocks = jnp.stack(columns).reshape(kk, ibk, 1, width, width)

    rows = slab // CORES
    term = jnp.stack(terms)
    share = rows * width // col_count
    shares = term.reshape(kk, col_count, share // 128, 128).transpose(1, 0, 2, 3)
    summed = jnp.sum(lax.all_to_all(shares, "col", 0, 0), axis=0)
    base = lax.dynamic_slice_in_dim(dinv, row_at * rows, rows, 1)
    base = base.reshape(kk, col_count, share // 128, 128)
    base = lax.dynamic_index_in_dim(base, col_at, 1, keepdims=False)
    piece = (base.astype(F32) - summed).astype(BF16)
    pieces = jnp.broadcast_to(piece[None], (col_count,) + piece.shape)
    pieces = lax.all_to_all(pieces, "col", 0, 0)
    half = pieces.transpose(1, 0, 2, 3).reshape(kk, rows, width)
    other = swap_cores(half, y_size)
    pair = jnp.stack([jnp.where(core == 0, half, other), jnp.where(core == 0, other, half)], axis=1)
    pair = pair.reshape(kk, slab, width).transpose(1, 0, 2)
    diagonal = gather_y(pair, y_at, y_size).transpose(1, 0, 2)
    return (column_blocks, diagonal)


def solution(mesh):
    placed = (P(None, "col", None, None, "row", None), P(None, None, "row", "col", None), P(), P())
    return jax.shard_map(
        body,
        mesh=mesh,
        in_specs=placed,
        out_specs=(P(None, None, "col", None, None), P()),
        check_vma=False,
    )
```

time: 546 us -> 259 us (0.47)
  waiting for transfers between devices: 466 us -> 141 us
  starting transfers between devices: 0.16 us -> 37.3 us
  other arithmetic: 21 us -> 12.5 us
    psum x3 -> x0, waiting for transfers between devices: 377 us -> none  [the longest x1 252 us: body(): summed = lax.psum(term, ('row', 'col'))]
    ppermute x0 -> x23, waiting for transfers between devices: none -> 36.3 us  [the longest x9 24 us: gather_y(): got = lax.ppermute(own, 'row', row_pairs(y_size, shift))]
    ppermute x0 -> x23, starting transfers between devices: none -> 20.4 us  [the longest x9 10.6 us: gather_y(): got = lax.ppermute(own, 'row', row_pairs(y_size, shift))]
    all_to_all x0 -> x3, waiting for transfers between devices: none -> 17.1 us  [the longest x1 10.2 us: body(): summed = jnp.sum(lax.all_to_all(shares, 'col', 0, 0), axis=0)]
    all_to_all x0 -> x3, starting transfers between devices: none -> 16.9 us  [the longest x1 7.19 us: body(): summed = jnp.sum(lax.all_to_all(shares, 'col', 0, 0), axis=0)]
    reshape x3 -> x5, local copies, waits for them, and re-layouts: 25.5 us -> 14.6 us  [the longest x1 13.5 us: body(): inverse = ainv.reshape(ibk, width, jbk * width)]
    convert_element_type x5 -> x1, other arithmetic: 9.64 us -> 0.01 us  [body(): piece = (base.astype(F32) - summed).astype(BF16)]
    select_n x2, other arithmetic: 10.4 us -> 3.09 us  [the longest x1 1.75 us: body(): own = jnp.where(keep_cols[:, :, None, None] > 0, own, jnp.zeros_like(own))]
  transfers between devices with their start and end apart: 4 -> 27, of which waited for: 4 -> 13; matrix products, arithmetic and copies ran while one was open for 9% -> 18% of each run, Pallas kernels for 0% -> 0%
where the time goes in v1:
time: 259 us; the launch traced here: 257 us
  waiting for transfers between devices  141 us (54%)
  starting transfers between devices  37.3 us (14%)
  local copies, waits for them, and re-layouts  31.8 us (12%)
  matrix products  18.1 us (7%)
  between operations  15.9 us (6%)
  other arithmetic  12.5 us (5%)
    all_gather x1, waiting for transfers between devices, gather_panel(): return lax.all_gather(own, 'col', axis=2, tiled=True).reshape(kk, -1, width)  87.6 us
    ppermute x9, waiting for transfers between devices, gather_y(): got = lax.ppermute(own, 'row', row_pairs(y_size, shift))  24 us
    reshape x1, local copies, waits for them, and re-layouts, body(): inverse = ainv.reshape(ibk, width, jbk * width)  13.5 us
    dot_general x2, matrix products, body(): both = jnp.dot(mine, masked[k], preferred_element_type=F32) + sent  11 us
    ppermute x6, waiting for transfers between devices, scatter_sum_y(): total = total + lax.ppermute(piece, 'row', row_pairs(y_size, shift))  10.9 us
    ppermute x9, starting transfers between devices, gather_y(): got = lax.ppermute(own, 'row', row_pairs(y_size, shift))  10.6 us
    all_to_all x1, waiting for transfers between devices, body(): summed = jnp.sum(lax.all_to_all(shares, 'col', 0, 0), axis=0)  10.2 us
    ppermute x6, starting transfers between devices, scatter_sum_y(): total = total + lax.ppermute(piece, 'row', row_pairs(y_size, shift))  8.31 us
  transfers between devices with their start and end apart: 27, of which 13 were waited for; matrix products, arithmetic and copies ran while one was open for 18% of the time, Pallas kernels for 0%

profile of v1, /device:TPU:2, one launch (start us, length us, event | category | flops | bytes accessed | tf_op | source)
XLA Modules:
  0.0 256.6 jit_solution(10246532168998612957)
XLA Ops:
  7.2 0.8 reshape.98
  8.1 0.2 fusion.34
  8.3 1.8 bitcast_select_fusion.1
  10.1 13.5 %reshape.97 = bf16[2,512,4096]{2,1,0:T(8,128)(2,1)} reshape(bf16[2,1,512,8,1,512]{5,3,4,2,1,0:T(8,128)(2,1)} %param.4) | data formatting | bytes 16777216 | tf_op jit(solution)/shard_map/reshape | solution.py:69
  23.6 87.6 %all-gather.2.cloned.1.call-done = bf16[2,8,512,512]{3,2,1,0:T(8,128)(2,1)} async-done(((bf16[2,8,16,512]{3,2,1,0:T(8,128)(2,1)}), bf16[2,8,512,512]{3,2,1,0:T(8,128)(2,1)}) %all-gather.2.cloned.1.call-update) | async-done | bytes 8388624 | tf_op jit(solution)/shard_map/all_gather | solution.py:47
  111.2 4.0 %fusion.38 = (bf16[1,8,512,512]{3,2,1,0:T(8,128)(2,1)S(1)}, bf16[1,8,512,512]{3,2,1,0:T(8,128)(2,1)S(1)}) fusion(bf16[2,8,512,512]{3,2,1,0:T(8,128)(2,1)} %all-gather.2.cloned.1.call-done), kind=kLoop, calls=%fused_computation.78 | loop fusion | bytes 16777216 | tf_op jit(solution)/shard_map/slice | solution.py:90
  115.2 3.9 %copy-done.1 = bf16[2,512,4096]{2,1,0:T(8,128)(2,1)S(1)} copy-done((bf16[2,512,4096]{2,1,0:T(8,128)(2,1)S(1)}, bf16[2,512,4096]{2,1,0:T(8,128)(2,1)}, u32[]{:S(2)}) %copy-start.1) | copy-done | bytes 8388632
  119.1 3.3 %fusion = f32[512,512]{1,0:T(8,128)} fusion(bf16[4096,512]{1,0:T(8,128)(2,1)S(1)} %bitcast.175, bf16[2,512,4096]{2,1,0:T(8,128)(2,1)S(1)} %copy-done.1, s32[]{:T(128)S(6)} %select_n.217), kind=kOutput, calls=%fused_computation | convolution fusion | flops 2147483648 | bytes 9437188 | tf_op jit(solution)/shard_map/dot_general | solution.py:89
  122.4 3.3 %fusion.2 = f32[512,512]{1,0:T(8,128)} fusion(bf16[4096,512]{1,0:T(8,128)(2,1)S(1)} %bitcast.173, bf16[2,512,4096]{2,1,0:T(8,128)(2,1)S(1)} %copy-done.1, s32[]{:T(128)S(6)} %select_n.217), kind=kOutput, calls=%fused_computation.2 | convolution fusion | flops 2147483648 | bytes 9437188 | tf_op jit(solution)/shard_map/dot_general | solution.py:89
  125.7 0.5 collective-permute-start
  126.3 0.6 constant_dynamic-slice_fusion.1
  128.2 1.7 constant_dynamic-slice_fusion.4
  129.9 1.3 copy.38
  131.2 0.5 copy.37
  131.8 6.2 %fusion.15 = f32[512,512]{1,0:T(8,128)S(1)} fusion(f32[512,512]{1,0:T(8,128)} %collective-permute-done.8, bf16[4096,512]{1,0:T(8,128)(2,1)} %bitcast.176, bf16[2,512,4096]{2,1,0:T(8,128)(2,1)} %reshape.97, s32[]{:T(128)S(6)} %select_n.210), kind=kOutput, calls=%fused_computation.14 | convolution fusion | flops 2147745792 | bytes 10485764 | tf_op jit(solution)/shard_map/dot_general | solution.py:90
  138.0 1.0 dynamic-slice_bitcast_fusion.2
  138.9 3.0 %collective-permute-start.10 = (f32[128,512]{1,0:T(8,128)S(1)}, f32[128,512]{1,0:T(8,128)S(1)}, u32[]{:S(2)}, u32[]{:S(2)}) collective-permute-start(f32[128,512]{1,0:T(8,128)S(1)} %get-tuple-element.21), channel_id=1, source_target_pairs={{0,128},{32,160},{64,192},{96,224},{128,0},{160,32},{192,64},{224,... | collective-permute-start | bytes 786440 | tf_op jit(solution)/shard_map/ppermute | solution.py:41
  142.0 4.8 %fusion.12 = f32[512,512]{1,0:T(8,128)S(1)} fusion(f32[512,512]{1,0:T(8,128)} %collective-permute-done, bf16[4096,512]{1,0:T(8,128)(2,1)S(1)} %bitcast.174, bf16[2,512,4096]{2,1,0:T(8,128)(2,1)} %reshape.97, s32[]{:T(128)S(6)} %select_n.210), kind=kOutput, calls=%fused_computation.13 | convolution fusion | flops 2147745792 | bytes 10485764 | tf_op jit(solution)/shard_map/dot_general | solution.py:90
  146.8 1.0 dynamic-slice_bitcast_fusion.5
  147.8 0.6 collective-permute-start.1
  148.4 2.0 collective-permute-start.2
  150.4 0.7 collective-permute-start.3
  151.1 1.4 collective-permute-start.11
  152.5 0.6 collective-permute-start.9
  153.1 1.3 bitcast_select_fusion
  154.5 1.1 copy.32
  155.5 4.2 %all-to-all-start = ((bf16[4,2,512,128]{2,3,1,0:T(8,128)(2,1)}), bf16[4,2,512,128]{2,3,1,0:T(8,128)(2,1)S(1)}, u32[]{:S(2)}, u32[]{:S(2)}) async-start(bf16[4,2,512,128]{2,3,1,0:T(8,128)(2,1)} %copy.32), calls=%async_computation | async-start | bytes 2097152 | tf_op jit(solution)/shard_map/all_to_all | solution.py:83
  159.7 10.9 %collective-permute-done.11 = f32[128,512]{1,0:T(8,128)} collective-permute-done((f32[128,512]{1,0:T(8,128)}, f32[128,512]{1,0:T(8,128)}, u32[]{:S(2)}, u32[]{:S(2)}) %collective-permute-start.11) | collective-permute-done | bytes 262176 | tf_op jit(solution)/shard_map/ppermute | solution.py:41
  170.7 1.3 bitcast_dynamic-update-slice_fusion.6
  172.1 1.3 bitcast_dynamic-update-slice_fusion.10
  173.4 0.6 collective-permute-start.4
  174.1 4.1 %collective-permute-start.5 = (bf16[128,512]{1,0:T(8,128)(2,1)S(1)}, bf16[128,512]{1,0:T(8,128)(2,1)S(1)}, u32[]{:S(2)}, u32[]{:S(2)}) collective-permute-start(bf16[128,512]{1,0:T(8,128)(2,1)S(1)} %get-tuple-element.3), channel_id=1, source_target_pairs={{0,128},{32,160},{64,192},{96,224},{128,0},{160,32},{192,64},{224,... | collective-permute-start | bytes 393224 | tf_op jit(solution)/shard_map/ppermute | solution.py:31
  178.2 1.1 collective-permute-start.6
  179.3 0.4 collective-permute-start.13
  179.7 3.9 %collective-permute-done.12 = bf16[128,512]{1,0:T(8,128)(2,1)S(1)} collective-permute-done((bf16[128,512]{1,0:T(8,128)(2,1)S(1)}, bf16[128,512]{1,0:T(8,128)(2,1)S(1)}, u32[]{:S(2)}, u32[]{:S(2)}) %collective-permute-start.12) | collective-permute-done | bytes 131104 | tf_op jit(solution)/shard_map/ppermute | solution.py:31
  183.7 7.2 %collective-permute-done.13 = bf16[128,512]{1,0:T(8,128)(2,1)S(1)} collective-permute-done((bf16[128,512]{1,0:T(8,128)(2,1)S(1)}, bf16[128,512]{1,0:T(8,128)(2,1)S(1)}, u32[]{:S(2)}, u32[]{:S(2)}) %collective-permute-start.13) | collective-permute-done | bytes 131104 | tf_op jit(solution)/shard_map/ppermute | solution.py:31
  190.9 1.1 collective-permute-done.14
  192.1 0.1 collective-permute-start.15
  192.3 0.2 fusion.39
  192.6 0.6 collective-permute-start.17
  193.1 0.2 fusion.40
  193.4 0.1 collective-permute-start.18
  193.5 0.7 collective-permute-done.17
  194.3 0.5 collective-permute-done.18
  194.9 0.7 maximum_bitcast_fusion.3
  195.6 7.2 %all-to-all-start.1 = ((f32[32,2,8,128]{3,2,1,0:T(8,128)}), f32[32,2,8,128]{3,2,1,0:T(8,128)S(1)}, u32[]{:S(2)}, u32[]{:S(2)}) async-start(f32[32,2,8,128]{3,2,1,0:T(8,128)} %maximum_bitcast_fusion.3), calls=%async_computation.1 | async-start | bytes 524288 | tf_op jit(solution)/shard_map/all_to_all | solution.py:107
  202.8 0.1 collective-permute-start.7
  203.0 1.1 select_bitcast_fusion.1
  204.1 10.2 %all-to-all-done.1 = f32[32,2,8,128]{3,2,1,0:T(8,128)S(1)} async-done(((f32[32,2,8,128]{3,2,1,0:T(8,128)}), f32[32,2,8,128]{3,2,1,0:T(8,128)S(1)}, u32[]{:S(2)}, u32[]{:S(2)}) %all-to-all-start.1) | async-done | bytes 262176 | tf_op jit(solution)/shard_map/all_to_all | solution.py:107
  214.4 0.7 broadcast_in_dim.70
  215.0 5.6 %all-to-all-start.2 = ((bf16[32,2,8,128]{3,2,1,0:T(8,128)(2,1)}), bf16[32,2,8,128]{3,2,1,0:T(8,128)(2,1)S(1)}, u32[]{:S(2)}, u32[]{:S(2)}) async-start(bf16[32,2,8,128]{3,2,1,0:T(8,128)(2,1)} %broadcast_in_dim.70), calls=%async_computation.2 | async-start | bytes 262144 | tf_op jit(solution)/shard_map/all_to_all | solution.py:113
  220.6 1.9 select_bitcast_fusion.3
  222.5 6.9 %all-to-all-done.2 = bf16[32,2,8,128]{3,2,1,0:T(8,128)(2,1)S(1)} async-done(((bf16[32,2,8,128]{3,2,1,0:T(8,128)(2,1)}), bf16[32,2,8,128]{3,2,1,0:T(8,128)(2,1)S(1)}, u32[]{:S(2)}, u32[]{:S(2)}) %all-to-all-start.2) | async-done | bytes 131104 | tf_op jit(solution)/shard_map/all_to_all | solution.py:113
  229.5 0.1 reshape.106
  229.6 0.1 collective-permute-start.19
  229.7 1.2 maximum_bitcast_fusion.1
  230.9 0.1 collective-permute-done.19
  231.1 0.3 collective-permute-start.20
  231.4 1.5 maximum_bitcast_fusion
  232.9 3.8 %collective-permute-start.21 = (bf16[128,2,512]{2,0,1:T(8,128)(2,1)S(1)}, bf16[128,2,512]{2,0,1:T(8,128)(2,1)S(1)}, u32[]{:S(2)}, u32[]{:S(2)}) collective-permute-start(bf16[128,2,512]{2,0,1:T(8,128)(2,1)S(1)} %bitcast.178), channel_id=1, source_target_pairs={{0,128},{32,160},{64,192},{96,224},{128,0},{160,32},{192,64},{224,... | collective-permute-start | bytes 786440 | tf_op jit(solution)/shard_map/ppermute | solution.py:31
  236.9 4.1 %collective-permute-done.20 = bf16[128,2,512]{2,0,1:T(8,128)(2,1)S(1)} collective-permute-done((bf16[128,2,512]{2,0,1:T(8,128)(2,1)S(1)}, bf16[128,2,512]{2,0,1:T(8,128)(2,1)S(1)}, u32[]{:S(2)}, u32[]{:S(2)}) %collective-permute-start.20) | collective-permute-done | bytes 262176 | tf_op jit(solution)/shard_map/ppermute | solution.py:31
  241.0 6.4 %collective-permute-done.21 = bf16[128,2,512]{2,0,1:T(8,128)(2,1)S(1)} collective-permute-done((bf16[128,2,512]{2,0,1:T(8,128)(2,1)S(1)}, bf16[128,2,512]{2,0,1:T(8,128)(2,1)S(1)}, u32[]{:S(2)}, u32[]{:S(2)}) %collective-permute-start.21) | collective-permute-done | bytes 262176 | tf_op jit(solution)/shard_map/ppermute | solution.py:31
  247.6 1.2 collective-permute-done.22
  248.8 1.0 copy-done.7
  (69 shorter events, 1.1 us)
Async XLA Ops:
  7.2 195.7 %copy-start = (bf16[2,512,512]{2,1,0:T(8,128)(2,1)S(1)}, bf16[2,512,512]{2,1,0:T(8,128)(2,1)}, u32[]{:S(2)}) copy-start(bf16[2,512,512]{2,1,0:T(8,128)(2,1)} %param.7) | copy-start | bytes 3145732
  7.2 104.0 %all-gather.2.cloned.1.call-start = ((), (), s32[]{:S(2)}) async-start(), calls=%async_computation.3 | async-start | bytes 8650752 | tf_op jit(solution)/shard_map/all_gather | solution.py:47
  111.2 7.9 %copy-start.1 = (bf16[2,512,4096]{2,1,0:T(8,128)(2,1)S(1)}, bf16[2,512,4096]{2,1,0:T(8,128)(2,1)}, u32[]{:S(2)}) copy-start(bf16[2,512,4096]{2,1,0:T(8,128)(2,1)} %reshape.97) | copy-start | bytes 25165828
  115.2 7.2 %copy-start.4 = (bf16[1,8,512,512]{3,2,1,0:T(8,128)(2,1)}, bf16[1,8,512,512]{3,2,1,0:T(8,128)(2,1)S(1)}, u32[]{:S(2)}) copy-start(bf16[1,8,512,512]{3,2,1,0:T(8,128)(2,1)S(1)} %get-tuple-element.9) | copy-start | bytes 12582916
  115.2 7.2 %copy-start.2 = (bf16[1,8,512,512]{3,2,1,0:T(8,128)(2,1)}, bf16[1,8,512,512]{3,2,1,0:T(8,128)(2,1)S(1)}, u32[]{:S(2)}) copy-start(bf16[1,8,512,512]{3,2,1,0:T(8,128)(2,1)S(1)} %get-tuple-element.8) | copy-start | bytes 12582916
  122.4 9.4 %collective-permute-start.8 = (f32[512,512]{1,0:T(8,128)}, f32[512,512]{1,0:T(8,128)}, u32[]{:S(2)}, u32[]{:S(2)}) collective-permute-start(f32[512,512]{1,0:T(8,128)} %fusion), channel_id=1, source_target_pairs={{0,32},{32,0},{64,96},{96,64},{128,160},{160,128},{192,224},{224,1... | collective-permute-start | bytes 3145736 | tf_op jit(solution)/shard_map/ppermute | solution.py:24
  122.4 3.8 %copy-start.9 = (s32[2,64]{1,0:T(2,128)S(1)}, s32[2,64]{1,0:T(2,128)}, u32[]{:S(2)}) copy-start(s32[2,64]{1,0:T(2,128)} %param.6) | copy-start | bytes 1540
  125.7 16.3 %collective-permute-start = (f32[512,512]{1,0:T(8,128)}, f32[512,512]{1,0:T(8,128)}, u32[]{:S(2)}, u32[]{:S(2)}) collective-permute-start(f32[512,512]{1,0:T(8,128)} %fusion.2), channel_id=1, source_target_pairs={{0,32},{32,0},{64,96},{96,64},{128,160},{160,128},{192,224},{224,1... | collective-permute-start | bytes 3145736 | tf_op jit(solution)/shard_map/ppermute | solution.py:24
  131.2 19.9 %collective-permute-start.16 = (bf16[2,512,512]{1,2,0:T(8,128)(2,1)}, bf16[2,512,512]{1,2,0:T(8,128)(2,1)}, u32[]{:S(2)}, u32[]{:S(2)}) collective-permute-start(bf16[2,512,512]{1,2,0:T(8,128)(2,1)} %bitcast.185), channel_id=1, source_target_pairs={{0,32},{32,0},{64,96},{96,64},{128,160},{160,128},{192,224},{224,1... | collective-permute-start | bytes 3145736 | tf_op jit(solution)/shard_map/ppermute | solution.py:24
  131.8 10.2 %copy-start.3 = (bf16[1,8,512,512]{3,2,1,0:T(8,128)(2,1)S(1)}, bf16[1,8,512,512]{3,2,1,0:T(8,128)(2,1)}, u32[]{:S(2)}) copy-start(bf16[1,8,512,512]{3,2,1,0:T(8,128)(2,1)} %copy-done.2) | copy-start | bytes 12582916
  138.0 4.0 %copy-start.6 = (f32[512,512]{1,0:T(8,128)}, f32[512,512]{1,0:T(8,128)S(1)}, u32[]{:S(2)}) copy-start(f32[512,512]{1,0:T(8,128)S(1)} %fusion.15) | copy-start | bytes 3145732
  138.9 13.6 %collective-permute-start.10 = (f32[128,512]{1,0:T(8,128)S(1)}, f32[128,512]{1,0:T(8,128)S(1)}, u32[]{:S(2)}, u32[]{:S(2)}) collective-permute-start(f32[128,512]{1,0:T(8,128)S(1)} %get-tuple-element.21), channel_id=1, source_target_pairs={{0,128},{32,160},{64,192},{96,224},{128,0},{160,32},{192,64},{224,... | collective-permute-start | bytes 786440 | tf_op jit(solution)/shard_map/ppermute | solution.py:41
  146.8 7.6 %copy-start.5 = (f32[512,512]{1,0:T(8,128)}, f32[512,512]{1,0:T(8,128)S(1)}, u32[]{:S(2)}) copy-start(f32[512,512]{1,0:T(8,128)S(1)} %fusion.12) | copy-start | bytes 3145732
  147.8 24.2 %collective-permute-start.1 = (f32[128,512]{1,0:T(8,128)}, f32[128,512]{1,0:T(8,128)}, u32[]{:S(2)}, u32[]{:S(2)}) collective-permute-start(f32[128,512]{1,0:T(8,128)} %get-tuple-element.14), channel_id=1, source_target_pairs={{0,64},{32,96},{64,128},{96,160},{128,192},{160,224},{192,0},{224,... | collective-permute-start | bytes 786440 | tf_op jit(solution)/shard_map/ppermute | solution.py:41
  148.4 23.7 %collective-permute-start.2 = (f32[128,512]{1,0:T(8,128)}, f32[128,512]{1,0:T(8,128)}, u32[]{:S(2)}, u32[]{:S(2)}) collective-permute-start(f32[128,512]{1,0:T(8,128)} %get-tuple-element.16), channel_id=1, source_target_pairs={{0,128},{32,160},{64,192},{96,224},{128,0},{160,32},{192,64},{224,... | collective-permute-start | bytes 786440 | tf_op jit(solution)/shard_map/ppermute | solution.py:41
  150.4 21.7 %collective-permute-start.3 = (f32[128,512]{1,0:T(8,128)S(1)}, f32[128,512]{1,0:T(8,128)}, u32[]{:S(2)}, u32[]{:S(2)}) collective-permute-start(f32[128,512]{1,0:T(8,128)S(1)} %get-tuple-element.15), channel_id=1, source_target_pairs={{0,192},{32,224},{64,0},{96,32},{128,64},{160,96},{192,128},{224,1... | collective-permute-start | bytes 786440 | tf_op jit(solution)/shard_map/ppermute | solution.py:41
  151.1 19.5 %collective-permute-start.11 = (f32[128,512]{1,0:T(8,128)}, f32[128,512]{1,0:T(8,128)}, u32[]{:S(2)}, u32[]{:S(2)}) collective-permute-start(f32[128,512]{1,0:T(8,128)} %get-tuple-element.20), channel_id=1, source_target_pairs={{0,192},{32,224},{64,0},{96,32},{128,64},{160,96},{192,128},{224,1... | collective-permute-start | bytes 786440 | tf_op jit(solution)/shard_map/ppermute | solution.py:41
  152.5 3.0 %copy-start.8 = (f32[128,512]{1,0:T(8,128)}, f32[128,512]{1,0:T(8,128)S(1)}, u32[]{:S(2)}) copy-start(f32[128,512]{1,0:T(8,128)S(1)} %collective-permute-done.10) | copy-start | bytes 786436
  152.5 18.1 %collective-permute-start.9 = (f32[128,512]{1,0:T(8,128)}, f32[128,512]{1,0:T(8,128)}, u32[]{:S(2)}, u32[]{:S(2)}) collective-permute-start(f32[128,512]{1,0:T(8,128)} %get-tuple-element.19), channel_id=1, source_target_pairs={{0,64},{32,96},{64,128},{96,160},{128,192},{160,224},{192,0},{224,... | collective-permute-start | bytes 786440 | tf_op jit(solution)/shard_map/ppermute | solution.py:41
  155.5 36.7 %all-to-all-start = ((bf16[4,2,512,128]{2,3,1,0:T(8,128)(2,1)}), bf16[4,2,512,128]{2,3,1,0:T(8,128)(2,1)S(1)}, u32[]{:S(2)}, u32[]{:S(2)}) async-start(bf16[4,2,512,128]{2,3,1,0:T(8,128)(2,1)} %copy.32), calls=%async_computation | async-start | bytes 2097152 | tf_op jit(solution)/shard_map/all_to_all | solution.py:83
  172.0 11.7 %collective-permute-start.12 = (bf16[128,512]{1,0:T(8,128)(2,1)S(1)}, bf16[128,512]{1,0:T(8,128)(2,1)S(1)}, u32[]{:S(2)}, u32[]{:S(2)}) collective-permute-start(bf16[128,512]{1,0:T(8,128)(2,1)S(1)} %get-tuple-element.5), channel_id=1, source_target_pairs={{0,64},{32,96},{64,128},{96,160},{128,192},{160,224},{192,0},{224,... | collective-permute-start | bytes 393224 | tf_op jit(solution)/shard_map/ppermute | solution.py:31
  173.4 18.7 %collective-permute-start.4 = (bf16[128,512]{1,0:T(8,128)(2,1)S(1)}, bf16[128,512]{1,0:T(8,128)(2,1)S(1)}, u32[]{:S(2)}, u32[]{:S(2)}) collective-permute-start(bf16[128,512]{1,0:T(8,128)(2,1)S(1)} %get-tuple-element.3), channel_id=1, source_target_pairs={{0,64},{32,96},{64,128},{96,160},{128,192},{160,224},{192,0},{224,... | collective-permute-start | bytes 393224 | tf_op jit(solution)/shard_map/ppermute | solution.py:31
  174.1 18.1 %collective-permute-start.5 = (bf16[128,512]{1,0:T(8,128)(2,1)S(1)}, bf16[128,512]{1,0:T(8,128)(2,1)S(1)}, u32[]{:S(2)}, u32[]{:S(2)}) collective-permute-start(bf16[128,512]{1,0:T(8,128)(2,1)S(1)} %get-tuple-element.3), channel_id=1, source_target_pairs={{0,128},{32,160},{64,192},{96,224},{128,0},{160,32},{192,64},{224,... | collective-permute-start | bytes 393224 | tf_op jit(solution)/shard_map/ppermute | solution.py:31
  178.2 14.0 %collective-permute-start.6 = (bf16[128,512]{1,0:T(8,128)(2,1)S(1)}, bf16[128,512]{1,0:T(8,128)(2,1)S(1)}, u32[]{:S(2)}, u32[]{:S(2)}) collective-permute-start(bf16[128,512]{1,0:T(8,128)(2,1)S(1)} %get-tuple-element.3), channel_id=1, source_target_pairs={{0,192},{32,224},{64,0},{96,32},{128,64},{160,96},{192,128},{224,1... | collective-permute-start | bytes 393224 | tf_op jit(solution)/shard_map/ppermute | solution.py:31
  179.3 11.6 %collective-permute-start.13 = (bf16[128,512]{1,0:T(8,128)(2,1)S(1)}, bf16[128,512]{1,0:T(8,128)(2,1)S(1)}, u32[]{:S(2)}, u32[]{:S(2)}) collective-permute-start(bf16[128,512]{1,0:T(8,128)(2,1)S(1)} %get-tuple-element.5), channel_id=1, source_target_pairs={{0,128},{32,160},{64,192},{96,224},{128,0},{160,32},{192,64},{224,... | collective-permute-start | bytes 393224 | tf_op jit(solution)/shard_map/ppermute | solution.py:31
  183.7 8.4 %collective-permute-start.14 = (bf16[128,512]{1,0:T(8,128)(2,1)S(1)}, bf16[128,512]{1,0:T(8,128)(2,1)S(1)}, u32[]{:S(2)}, u32[]{:S(2)}) collective-permute-start(bf16[128,512]{1,0:T(8,128)(2,1)S(1)} %get-tuple-element.5), channel_id=1, source_target_pairs={{0,192},{32,224},{64,0},{96,32},{128,64},{160,96},{192,128},{224,1... | collective-permute-start | bytes 393224 | tf_op jit(solution)/shard_map/ppermute | solution.py:31
  192.1 11.0 %collective-permute-start.15 = (bf16[512,512]{1,0:T(8,128)(2,1)S(1)}, bf16[512,512]{1,0:T(8,128)(2,1)}, u32[]{:S(2)}, u32[]{:S(2)}) collective-permute-start(bf16[512,512]{1,0:T(8,128)(2,1)S(1)} %bitcast.168), channel_id=1, source_target_pairs={{0,32},{32,0},{64,96},{96,64},{128,160},{160,128},{192,224},{224,1... | collective-permute-start | bytes 1572872 | tf_op jit(solution)/shard_map/ppermute | solution.py:24
  192.6 1.7 collective-permute-start.17
  193.4 1.4 collective-permute-start.18
  195.6 18.7 %all-to-all-start.1 = ((f32[32,2,8,128]{3,2,1,0:T(8,128)}), f32[32,2,8,128]{3,2,1,0:T(8,128)S(1)}, u32[]{:S(2)}, u32[]{:S(2)}) async-start(f32[32,2,8,128]{3,2,1,0:T(8,128)} %maximum_bitcast_fusion.3), calls=%async_computation.1 | async-start | bytes 524288 | tf_op jit(solution)/shard_map/all_to_all | solution.py:107
  202.8 17.8 %collective-permute-start.7 = (bf16[512,512]{1,0:T(8,128)(2,1)S(1)}, bf16[512,512]{1,0:T(8,128)(2,1)}, u32[]{:S(2)}, u32[]{:S(2)}) collective-permute-start(bf16[512,512]{1,0:T(8,128)(2,1)S(1)} %bitcast.171), channel_id=1, source_target_pairs={{0,32},{32,0},{64,96},{96,64},{128,160},{160,128},{192,224},{224,1... | collective-permute-start | bytes 1572872 | tf_op jit(solution)/shard_map/ppermute | solution.py:24
  215.0 14.4 %all-to-all-start.2 = ((bf16[32,2,8,128]{3,2,1,0:T(8,128)(2,1)}), bf16[32,2,8,128]{3,2,1,0:T(8,128)(2,1)S(1)}, u32[]{:S(2)}, u32[]{:S(2)}) async-start(bf16[32,2,8,128]{3,2,1,0:T(8,128)(2,1)} %broadcast_in_dim.70), calls=%async_computation.2 | async-start | bytes 262144 | tf_op jit(solution)/shard_map/all_to_all | solution.py:113
  229.6 1.4 collective-permute-start.19
  231.1 9.9 %collective-permute-start.20 = (bf16[128,2,512]{2,0,1:T(8,128)(2,1)S(1)}, bf16[128,2,512]{2,0,1:T(8,128)(2,1)S(1)}, u32[]{:S(2)}, u32[]{:S(2)}) collective-permute-start(bf16[128,2,512]{2,0,1:T(8,128)(2,1)S(1)} %bitcast.177), channel_id=1, source_target_pairs={{0,64},{32,96},{64,128},{96,160},{128,192},{160,224},{192,0},{224,... | collective-permute-start | bytes 786440 | tf_op jit(solution)/shard_map/ppermute | solution.py:31
  232.9 14.6 %collective-permute-start.21 = (bf16[128,2,512]{2,0,1:T(8,128)(2,1)S(1)}, bf16[128,2,512]{2,0,1:T(8,128)(2,1)S(1)}, u32[]{:S(2)}, u32[]{:S(2)}) collective-permute-start(bf16[128,2,512]{2,0,1:T(8,128)(2,1)S(1)} %bitcast.178), channel_id=1, source_target_pairs={{0,128},{32,160},{64,192},{96,224},{128,0},{160,32},{192,64},{224,... | collective-permute-start | bytes 786440 | tf_op jit(solution)/shard_map/ppermute | solution.py:31
  236.8 12.0 %collective-permute-start.22 = (bf16[128,2,512]{2,0,1:T(8,128)(2,1)S(1)}, bf16[128,2,512]{2,0,1:T(8,128)(2,1)S(1)}, u32[]{:S(2)}, u32[]{:S(2)}) collective-permute-start(bf16[128,2,512]{2,0,1:T(8,128)(2,1)S(1)} %bitcast.179), channel_id=1, source_target_pairs={{0,192},{32,224},{64,0},{96,32},{128,64},{160,96},{192,128},{224,1... | collective-permute-start | bytes 786440 | tf_op jit(solution)/shard_map/ppermute | solution.py:31
  248.8 1.0 copy-start.7
Sparse Core Ops, SparseCore 0:
  11.2 99.9 all-gather.1
